TPU v7x, 256 devices: a whole 4x4x8 slice. The times are simulated.
256 devices in a mesh: grp: 8 (over x, y_lo), head: 32 (over y_hi, z, core).
Axes of the slice: x: 4, y: 4 (y_hi: 2, y_lo: 2; y = y_hi * 2 + y_lo), z: 8, core: 2. Of those that a mesh axis runs over, the one named last changes fastest.
Arguments:
- kv_pool: bfloat16 [2, 352, 128, 12288], P(None, 'grp', None, 'head'), may hold values from -6 to 6
- qkv_new: bfloat16 [3, 4, 256, 12288], P(None, None, 'grp', 'head'), may hold values from -119 to 119
- w_out: bfloat16 [12288, 6144], P('head'), may hold values from -0.109375 to 0.109375
- table: int32 [256, 4], P('grp'), may hold values from 0 to 43, as said below
- lengths: int32 [256], replicated, may hold values from 0 to 512, as said below
- migration: int32 [16, 2], replicated, may hold values from 0 to 30, as said below
Outputs:
- mixed: bfloat16 [4, 256, 6144], P(None, 'grp', 'head')
Inputs may be any that keep to these rules, and one draw needn't show every extreme that they name: `table`: within a group, the pages of resident slots' first ceil(length / 128) entries are distinct numbers below 36; later entries repeat the last used page; landing slots' rows are 36 + m * 4 + j. Landing slots have length 0. In each pair of partner groups exactly one moves out 2 of its resident requests, whose lengths exceed (3) * 128; all other resident lengths are at most 128. `migration`: rows of a group that moves: distinct resident slots and arrivals in 0 to 3; rows of the other group: slot 30 and arrival 0.
All inputs are finite; a program needn't handle non-finite values.
Results may differ from a plain program's by a relative error of at most 0.02.
Values may be sent and summed in bfloat16 or wider, within the bound.
A program may use at most 128 MiB of HBM per device.

v0:
```python
import jax
import jax.numpy as jnp
from jax import lax
from jax.sharding import PartitionSpec as P

HD = 128


def partner_2(block, axis, distance):
    count = lax.axis_size(axis)
    route = []
    for low in range(count):
        high = low | 1 << distance
        if high != low and high < count:
            route += [(low, high), (high, low)]
    return lax.ppermute(block, axis, route)


def key_mask(page_rows, row_len, page_count, page_len):
    page_slot = jnp.arange(page_rows.shape[1], dtype=jnp.int32)
    page_need = (row_len + page_len - 1) // page_len
    used = page_slot[None, :] < page_need[:, None]
    page_ids = jnp.arange(page_count, dtype=jnp.int32)
    matched = (page_rows[:, :, None] == page_ids[None, None, :]) & used[:, :, None]
    first_pos = jnp.sum(jnp.where(matched, page_slot[None, :, None] * page_len + 1, 0), axis=1)
    in_page = jnp.arange(page_len, dtype=jnp.int32)
    key_pos = first_pos[:, :, None] - 1 + in_page[None, None, :]
    key_valid = (first_pos[:, :, None] > 0) & (key_pos < row_len[:, None, None])
    return key_valid.reshape(page_rows.shape[0], page_count * page_len)


def attend(queries, cache_keys, cache_vals, key_valid, new_keys, new_vals, shared):
    scale = HD ** (-0.5)
    if shared:
        cache_score = jnp.einsum(
            "snhd,khd->hsnk", queries, cache_keys, preferred_element_type=jnp.float32
        )
    else:
        cache_score = jnp.einsum(
            "snhd,nkhd->hsnk", queries, cache_keys, preferred_element_type=jnp.float32
        )
    cache_score = jnp.where(key_valid[None, None], cache_score * scale, -jnp.inf)
    new_score = (
        jnp.einsum("snhd,unhd->hsnu", queries, new_keys, preferred_element_type=jnp.float32) * scale
    )
    step_ids = jnp.arange(queries.shape[0], dtype=jnp.int32)
    causal = step_ids[:, None] >= step_ids[None, :]
    new_score = jnp.where(causal[None, :, None, :], new_score, -jnp.inf)
    top_score = jnp.maximum(jnp.max(cache_score, -1), jnp.max(new_score, -1))
    cache_exp = jnp.exp(cache_score - top_score[..., None])
    new_exp = jnp.exp(new_score - top_score[..., None])
    total = jnp.sum(cache_exp, -1) + jnp.sum(new_exp, -1)
    cache_wts = (cache_exp / total[..., None]).astype(jnp.bfloat16)
    new_wts = (new_exp / total[..., None]).astype(jnp.bfloat16)
    if shared:
        mixed_out = jnp.einsum(
            "hsnk,khd->snhd", cache_wts, cache_vals, preferred_element_type=jnp.float32
        )
    else:
        mixed_out = jnp.einsum(
            "hsnk,nkhd->snhd", cache_wts, cache_vals, preferred_element_type=jnp.float32
        )
    mixed_out = mixed_out + jnp.einsum(
        "hsnu,unhd->snhd", new_wts, new_vals, preferred_element_type=jnp.float32
    )
    return mixed_out.astype(jnp.bfloat16)


def per_device(kv_pool, qkv_new, w_out, table, lengths, migration):
    step_count = qkv_new.shape[1]
    slot_count = table.shape[0]
    page_count = kv_pool.shape[1]
    page_len = kv_pool.shape[2]
    feat_width = kv_pool.shape[3]
    head_count = feat_width // HD
    group_count = lax.axis_size("grp")
    move_count = migration.shape[0] // group_count
    live_slots = slot_count - move_count
    swap_bit = group_count.bit_length() - 2
    grp_index = lax.axis_index("grp")
    partner = jnp.bitwise_xor(grp_index, group_count // 2)
    all_len = lengths.reshape(group_count, slot_count)
    all_plan = migration.reshape(group_count, move_count, 2)
    own_len = jnp.take(all_len, grp_index, axis=0)
    own_plan = jnp.take(all_plan, grp_index, axis=0)
    part_plan = jnp.take(all_plan, partner, axis=0)
    part_len = jnp.take(all_len, partner, axis=0)
    split_new = qkv_new.reshape(3, step_count, slot_count, head_count, HD)
    pool_keys = kv_pool[0].reshape(page_count * page_len, head_count, HD)
    pool_vals = kv_pool[1].reshape(page_count * page_len, head_count, HD)
    step_ids = jnp.arange(step_count, dtype=jnp.int32)
    slot_ids = jnp.arange(slot_count, dtype=jnp.int32)
    key_valid = key_mask(table, own_len, page_count, page_len)
    own_attn = attend(
        split_new[0], pool_keys, pool_vals, key_valid, split_new[1], split_new[2], True
    )
    leave_step = jnp.min(
        jnp.where(own_plan[None, :, 0] == slot_ids[:, None], own_plan[None, :, 1], step_count),
        axis=1,
    )
    stay_mask = (step_ids[:, None] < leave_step[None, :]) & (slot_ids[None, :] < live_slots)
    own_attn = jnp.where(stay_mask[:, :, None, None], own_attn, jnp.zeros_like(own_attn))
    part_slot = part_plan[:, 0]
    part_arr = part_plan[:, 1]
    is_moved = part_slot < live_slots
    before = step_ids[:, None] < part_arr[None, :]
    land_new = qkv_new[:, :, live_slots:]
    out_slot = own_plan[:, 0]
    page_rows = jnp.take(table, out_slot, axis=0)
    sent_pages = jnp.take(kv_pool, page_rows.reshape(-1), axis=1)
    sent_pages = sent_pages.reshape(2 * move_count * page_rows.shape[1] * page_len, feat_width)
    sent_new = jnp.take(qkv_new[1:3], out_slot, axis=2).reshape(
        2 * step_count * move_count, feat_width
    )
    received = partner_2(jnp.concatenate([sent_pages, sent_new], 0), "grp", swap_bit)
    page_rows_count = sent_pages.shape[0]
    got_pages = received[:page_rows_count].reshape(
        2, move_count, page_rows.shape[1] * page_len, head_count, HD
    )
    got_new = received[page_rows_count:].reshape(2, step_count, move_count, feat_width)
    history = jnp.where(before[None, :, :, None], got_new, land_new[1:3])
    history = history.reshape(2, step_count, move_count, head_count, HD)
    moved_len = jnp.take(part_len, part_slot)
    moved_valid = (
        jnp.arange(page_rows.shape[1] * page_len, dtype=jnp.int32)[None, :] < moved_len[:, None]
    )
    land_attn = attend(
        split_new[0][:, live_slots:],
        got_pages[0],
        got_pages[1],
        moved_valid,
        history[0],
        history[1],
        False,
    )
    served = is_moved[None, :] & jnp.logical_not(before)
    land_attn = jnp.where(served[:, :, None, None], land_attn, jnp.zeros_like(land_attn))
    attn = jnp.concatenate([own_attn[:, :live_slots], land_attn], 1)
    attn_rows = attn.reshape(step_count * slot_count, feat_width)
    partial_value = jnp.dot(attn_rows, w_out, preferred_element_type=jnp.float32)
    summed = lax.psum_scatter(
        partial_value.astype(jnp.bfloat16), "head", scatter_dimension=1, tiled=True
    ).astype(jnp.float32)
    return summed.astype(jnp.bfloat16).reshape(step_count, slot_count, summed.shape[1])


def solution(mesh):
    return jax.shard_map(
        per_device,
        mesh=mesh,
        in_specs=(
            P(None, "grp", None, "head"),
            P(None, None, "grp", "head"),
            P("head", None),
            P("grp", None),
            P(),
            P(),
        ),
        out_specs=P(None, "grp", "head"),
        check_vma=False,
    )
```

profile of v0, /device:TPU:2, one launch (start us, length us, event | category | flops | bytes accessed | tf_op | source)
XLA Modules:
  0.0 207.5 jit_solution(11490663098990786845)
XLA Ops:
  6.5 0.8 reshape.314
  7.3 0.8 reshape.313
  8.1 0.1 copy.206
  8.2 0.1 fusion.46
  8.3 0.6 gather_fusion.3
  8.9 0.1 copy.212
  9.0 0.1 copy.190
  9.1 0.1 and_reduce_fusion
  9.3 0.7 fusion.42
  10.0 0.8 copy.207
  10.7 0.6 gather_fusion
  11.3 0.1 broadcast_select_fusion.4
  11.4 0.1 select_n.133
  11.4 0.1 select_n.131
  11.5 0.9 slice.78
  12.5 0.1 copy.244
  12.6 0.6 gather_fusion.2
  13.2 0.1 broadcast_in_dim.209
  13.3 4.3 %gather_fusion.1 = bf16[8,2,128,384]{3,2,1,0:T(8,128)(2,1)S(1)} fusion(bf16[2,44,128,384]{3,2,1,0:T(8,128)(2,1)} %param.10, s32[1024]{0:T(1024)S(1)} %pad_clamp_fusion.1), kind=kCustom, calls=%fused_computation.1 | custom fusion | bytes 3145760 | tf_op jit(solution)/shard_map/jit(_take)/gather | solution.py:110
  17.7 0.2 copy.208
  17.9 0.1 broadcast_bitcast_fusion
  18.0 0.1 broadcast_select_fusion.1
  18.0 0.6 bitcast_select_fusion
  18.7 1.3 pad_maximum_fusion
  20.0 2.1 %collective-permute-start = (bf16[2064,384]{1,0:T(8,128)(2,1)}, bf16[2064,384]{1,0:T(8,128)(2,1)S(1)}, u32[]{:S(2)}, u32[]{:S(2)}) collective-permute-start(bf16[2064,384]{1,0:T(8,128)(2,1)} %pad_maximum_fusion), channel_id=1, source_target_pairs={{0,128},{128,0},{32,160},{160,32},{64,192},{192,64},{96,224},{224,... | collective-permute-start | bytes 4755464 | tf_op jit(solution)/shard_map/ppermute | solution.py:16
  22.1 0.1 compare_reduce_fusion
  22.3 4.0 %fusion.49 = (bf16[1,44,128,384]{3,2,1,0:T(8,128)(2,1)}, bf16[1,44,128,384]{3,2,1,0:T(8,128)(2,1)}) fusion(bf16[2,44,128,384]{3,2,1,0:T(8,128)(2,1)S(1)} %copy-done.1), kind=kLoop, calls=%fused_computation.112 | loop fusion | bytes 17301504 | tf_op jit(solution)/shard_map/slice | solution.py:90
  26.3 0.1 select_reduce_fusion
  26.5 0.6 not_and_fusion
  27.1 0.1 copy.217
  27.2 0.1 copy.195
  27.3 0.7 copy.216
  28.0 0.1 iota_compare_fusion.1
  28.1 0.2 fusion.25
  28.3 0.1 copy.196
  28.5 11.9 %reshape.444 = bf16[5632,3,128]{2,1,0:T(4,128)(2,1)} reshape(bf16[1,44,128,384]{3,2,1,0:T(8,128)(2,1)} %get-tuple-element.37) | data formatting | bytes 8650752 | tf_op jit(solution)/shard_map/reshape;squeeze | solution.py:89
  40.4 0.1 fusion.32
  40.5 0.3 add.102
  40.7 0.3 and.84
  41.0 0.3 fusion.18
  41.3 5.2 %fusion.55 = (f32[3,4,32]{2,1,0:T(4,128)S(1)}, f32[3,4,32,5632]{3,2,1,0:T(8,128)S(1)}) fusion(bf16[5632,3,128,1]{2,1,0,3:T(4,128)(2,1)} %bitcast.75, bf16[4,32,3,128]{3,2,1,0:T(4,128)(2,1)S(1)} %squeeze.24, pred[32,5632]{1,0:T(8,128)(4,1)S(1)} %fusion.18), kind=kOutput, calls=%fused_computation.118 | convolution fusion | flops 560135808 | bytes 13256192 | tf_op jit(solution)/shard_map/snhd,khd->hsnk/dot_general | solution.py:35
  46.5 0.1 fusion.31
  46.6 1.3 fusion.1
  48.0 1.8 copy-done
  49.8 0.1 divide_convert_fusion.5
  49.9 0.2 copy.203
  50.1 0.2 fusion.23
  50.4 11.9 %reshape.445 = bf16[5632,3,128]{2,1,0:T(4,128)(2,1)} reshape(bf16[1,44,128,384]{3,2,1,0:T(8,128)(2,1)} %get-tuple-element.36) | data formatting | bytes 8650752 | tf_op jit(solution)/shard_map/reshape;squeeze | solution.py:90
  62.3 0.1 fusion.41
  62.4 7.0 %fusion.5 = f32[4,32,3,128]{3,1,0,2:T(8,128)S(1)} fusion(bf16[5632,3,128,1]{2,1,0,3:T(4,128)(2,1)} %bitcast.77, f32[3,4,32,5632]{3,2,1,0:T(8,128)} %copy-done, f32[3,4,32]{2,1,0:T(4,128)S(1)} %add.108, f32[3,4,32]{2,1,0:T(4,128)S(1)} %max.14), kind=kOutput, calls=%fused_computation.15 | convolution fusion | flops 560136192 | bytes 13175808 | tf_op jit(solution)/shard_map/hsnk,khd->snhd/dot_general | solution.py:56
  69.4 0.7 fusion.20
  70.2 0.1 broadcast_select_fusion
  70.3 0.2 fusion.50
  70.5 0.3 reshape.447
  70.8 0.8 fusion.54
  71.6 0.4 fusion.53
  72.0 0.2 fusion.29
  72.2 0.3 reshape.446
  72.5 0.2 fusion.34
  72.7 0.9 fusion.14
  73.6 0.1 copy.224
  73.7 5.4 %convolution_convert_fusion = bf16[128,6144]{0,1:T(8,128)(2,1)} fusion(bf16[384,6144]{1,0:T(8,128)(2,1)} %param.12, bf16[16,8,3,128]{3,2,1,0:T(4,128)(2,1)S(1)} %bitcast.81), kind=kOutput, calls=%fused_computation.9 | convolution fusion | flops 604766208 | bytes 6389760 | tf_op jit(solution)/shard_map/dot_general | solution.py:140
  79.2 119.9 %reduce-scatter.2.cloned.1.call-done = bf16[128,192]{0,1:T(8,128)(2,1)} async-done(((bf16[128,6144]{0,1:T(8,128)(2,1)}), bf16[128,192]{0,1:T(8,128)(2,1)}) %reduce-scatter.2.cloned.1.call-update) | async-done | bytes 49168 | tf_op jit(solution)/shard_map/reduce_scatter | solution.py:141
  199.1 1.5 copy.225
  (54 shorter events, 0.5 us)
Async XLA Ops:
  6.5 192.6 %reduce-scatter.2.cloned.1.call-start = ((), (), s32[]{:S(2)}) async-start(), calls=%async_computation.1 | async-start | bytes 1622016 | tf_op jit(solution)/shard_map/reduce_scatter | solution.py:141
  17.7 4.6 %copy-start.2 = (bf16[3,4,32,384]{3,2,1,0:T(8,128)(2,1)S(1)}, bf16[3,4,32,384]{3,2,1,0:T(8,128)(2,1)}, u32[]{:S(2)}) copy-start(bf16[3,4,32,384]{3,2,1,0:T(8,128)(2,1)} %param.11) | copy-start | bytes 884740
  17.7 4.6 %copy-start.1 = (bf16[2,44,128,384]{3,2,1,0:T(8,128)(2,1)S(1)}, bf16[2,44,128,384]{3,2,1,0:T(8,128)(2,1)}, u32[]{:S(2)}) copy-start(bf16[2,44,128,384]{3,2,1,0:T(8,128)(2,1)} %param.10) | copy-start | bytes 25952260
  20.0 50.2 %collective-permute-start = (bf16[2064,384]{1,0:T(8,128)(2,1)}, bf16[2064,384]{1,0:T(8,128)(2,1)S(1)}, u32[]{:S(2)}, u32[]{:S(2)}) collective-permute-start(bf16[2064,384]{1,0:T(8,128)(2,1)} %pad_maximum_fusion), channel_id=1, source_target_pairs={{0,128},{128,0},{32,160},{160,32},{64,192},{192,64},{96,224},{224,... | collective-permute-start | bytes 4755464 | tf_op jit(solution)/shard_map/ppermute | solution.py:16
  22.3 4.0 %copy-start.4 = (s32[32,4]{0,1:T(4,128)S(1)}, s32[32,4]{0,1:T(4,128)}, u32[]{:S(2)}) copy-start(s32[32,4]{0,1:T(4,128)} %param.13) | copy-start | bytes 1540
  22.3 5.7 %copy-start.5 = (s32[2]{0:T(128)S(1)}, s32[2]{0:T(128)}, u32[]{:S(2)}) copy-start(s32[2]{0:T(128)} %get-tuple-element.32) | copy-start | bytes 28
  46.5 3.3 %copy-start = (f32[3,4,32,5632]{3,2,1,0:T(8,128)}, f32[3,4,32,5632]{3,2,1,0:T(8,128)S(1)}, u32[]{:S(2)}) copy-start(f32[3,4,32,5632]{3,2,1,0:T(8,128)S(1)} %get-tuple-element.54) | copy-start | bytes 25952260
  50.4 11.9 %copy-start.6 = (s32[2]{0:T(128)S(1)}, s32[2]{0:T(128)}, u32[]{:S(2)}) copy-start(s32[2]{0:T(128)} %get-tuple-element.55) | copy-start | bytes 28
  50.4 11.9 %copy-start.7 = (s32[2]{0:T(128)S(1)}, s32[2]{0:T(128)}, u32[]{:S(2)}) copy-start(s32[2]{0:T(128)} %get-tuple-element.57) | copy-start | bytes 28
  70.3 3.2 %copy-start.3 = (bf16[4,30,3,128]{3,1,0,2:T(8,128)(2,1)S(1)}, bf16[4,30,3,128]{3,1,0,2:T(8,128)(2,1)}, u32[]{:S(2)}) copy-start(bf16[4,30,3,128]{3,1,0,2:T(8,128)(2,1)} %fusion.20) | copy-start | bytes 276484
Sparse Core Ops, SparseCore 0:
  79.3 119.7 reduce-scatter.1
where the time goes:
time: 208 us; the launch traced here: 207 us
  waiting for transfers between devices  120 us (58%)
  local copies, waits for them, and re-layouts  44.1 us (21%)
  matrix products  20.4 us (10%)
  between operations  13.8 us (7%)
  other arithmetic  7.12 us (3%)
  starting transfers between devices  2.13 us (1%)
    reduce_scatter x1, waiting for transfers between devices, per_device(): lax.psum_scatter(partial_value.astype(jnp.bfloat16), 'head', scatter_dime...  120 us
    another operation x1, local copies, waits for them, and re-layouts, per_device(): pool_keys = kv_pool[0].reshape(page_count * page_len, head_count, HD)  11.9 us
    another operation x1, local copies, waits for them, and re-layouts, per_device(): pool_vals = kv_pool[1].reshape(page_count * page_len, head_count, HD)  11.9 us
    dot_general x1, matrix products, attend(): jnp.einsum('hsnk,khd->snhd', cache_wts, cache_vals, preferred_element_typ...  7.02 us
    dot_general x1, matrix products, per_device(): jnp.dot(attn_rows, w_out, preferred_element_type=jnp.float32)  5.44 us
    dot_general x1, matrix products, attend(): jnp.einsum('snhd,khd->hsnk', queries, cache_keys, preferred_element_type=...  5.15 us
    gather x2, local copies, waits for them, and re-layouts, per_device(): sent_pages = jnp.take(kv_pool, page_rows.reshape(-1), axis=1)  4.52 us
  transfers between devices with their start and end apart: 2, of which 1 were waited for; matrix products, arithmetic and copies ran while one was open for 22% of the time, Pallas kernels for 0%

commit v1 on v0

v1 whole, which is shorter than its diff:
```python
import jax
import jax.numpy as jnp
from jax import lax
from jax.experimental import pallas as pl
from jax.experimental.pallas import tpu as pltpu
from jax.sharding import PartitionSpec as P

MESH = pl.DeviceIdType.MESH
HD = 128
HEADS = 3
FEAT = HEADS * HD
STEPS = 4
SLOTS = 32
LIVE = 30
LIVE_PAGES = 36
PAGE = 128
MAXP = 4
ROWS = STEPS * SLOTS
RPS = 16
CHUNKS = 4
NZ = 8
Z_ORDER = (4, 3, 5, 2, 6, 1, 7, 0)
UNIT = 192
F32 = jnp.float32
BF16 = jnp.bfloat16
SCALE = HD ** -0.5


def iota(shape, dim):
    return lax.broadcasted_iota(jnp.int32, shape, dim)


def one_hot(cond):
    return jnp.where(cond, 1.0, 0.0).astype(BF16)


def dot(a, b):
    return jnp.dot(a, b, preferred_element_type=F32)


def dot_t(a, b):
    return lax.dot_general(a, b, (((1,), (1,)), ((), ())), preferred_element_type=F32)


def kernel(kv, qkv, w, table, lens, plan, out,
           kbuf, vbuf, wbuf, ext, land_src, land_dst, moved_src, moved_dst,
           qb, sc, sn, scm, snm, pc, pn, on, ob, attn,
           own, core_src, core_dst, y_src, y_dst, z_src, z_dst,
           k_sem, v_sem, w_sem, q_sem, land_sem, moved_sem, core_ssem, core_rsem, y_ssem, y_rsem, z_ssem, z_rsem):
    g = lax.axis_index("grp")
    h = lax.axis_index("head")
    yh, z, core = h // 16, lax.rem(h // 2, NZ), lax.rem(h, 2)
    sibling = (g, h + 1 - 2 * core)
    y_peer = (g, lax.rem(h + 16, 32))
    x_peer = (lax.rem(g + 4, 8), h)

    def z_peer(d):
        return (g, yh * 16 + lax.rem(z + d, NZ) * 2 + core)

    q_copy = pltpu.make_async_copy(qkv, ext.at[:, pl.ds(0, ROWS)], q_sem)
    q_copy.start()
    per = LIVE_PAGES // CHUNKS

    def page_copies(which, buf, sem):
        return [pltpu.make_async_copy(kv.at[which, pl.ds(n * per, per)], buf.at[pl.ds(n * per, per)], sem.at[n])
                for n in range(CHUNKS)]

    k_copies = page_copies(0, kbuf, k_sem)
    v_copies = page_copies(1, vbuf, v_sem)
    for cp in k_copies + v_copies:
        cp.start()

    barrier = pltpu.get_barrier_semaphore()
    peers = [sibling, y_peer, x_peer] + [z_peer(d) for d in range(1, NZ)]
    for peer in peers:
        pl.semaphore_signal(barrier, inc=1, device_id=peer, device_id_type=MESH)

    def w_copies(k):
        u, d = k // NZ, Z_ORDER[k % NZ]
        b = (1 - yh) if u == 0 else yh
        base = (b * NZ + lax.rem(z + d, NZ)) * FEAT
        res = []
        for n, tile in enumerate((2 * core, 1, 2 - 2 * core)):
            col = pl.multiple_of(base + tile * HD, HD)
            res.append(pltpu.make_async_copy(w.at[:, pl.ds(col, HD)], wbuf.at[k, :, pl.ds(n * HD, HD)], w_sem.at[k, n]))
        return res

    pair = lax.rem(g + 4, 8)
    mv_slot = [plan[0, g * 2 + m] for m in range(2)]
    mv_arr = [plan[1, g * 2 + m] for m in range(2)]
    in_slot = [plan[0, pair * 2 + m] for m in range(2)]
    in_arr = [plan[1, pair * 2 + m] for m in range(2)]
    mv_row = [jnp.minimum(s, LIVE - 1) for s in mv_slot]

    def pick(m, values):
        return jnp.where(m == 0, values[0], values[1])

    q_copy.wait()
    r, c = iota((16, ROWS), 0), iota((16, ROWS), 1)
    land_pick = one_hot((r < 8) & (c == (r & 3) * SLOTS + LIVE + (r >> 2)))
    for n in range(3):
        land_src[n] = dot(land_pick, ext[n, 0:ROWS]).astype(BF16)
        ext[n, ROWS + 16:256] = jnp.zeros((112, FEAT), BF16)

    live_rows = LIVE * RPS
    r, c = iota((live_rows, ROWS), 0), iota((live_rows, ROWS), 1)
    q_pick = one_hot(c == (r & 3) * SLOTS + (r >> 4))
    spread = dot(q_pick, ext[0, 0:ROWS])
    r, c = iota((live_rows, FEAT), 0), iota((live_rows, FEAT), 1)
    qb[0:live_rows] = jnp.where((c >> 7) == ((r >> 2) & 3), spread, 0.0).astype(BF16)

    r, c = iota((live_rows, ROWS), 0), iota((live_rows, ROWS), 1)
    raw = dot_t(qb[0:live_rows], ext[1, 0:ROWS])
    sn[...] = jnp.where(((c & 31) == (r >> 4)) & ((c >> 5) <= (r & 3)), raw * SCALE, -jnp.inf)

    pl.semaphore_wait(barrier, len(peers))
    land_copy = pltpu.make_async_remote_copy(
        src_ref=land_src, dst_ref=land_dst, send_sem=land_sem.at[0], recv_sem=land_sem.at[1],
        device_id=x_peer, device_id_type=MESH)
    land_copy.start()

    for cp in k_copies:
        cp.wait()
    for k in range(2 * NZ):
        for cp in w_copies(k):
            cp.start()
    lane = iota((RPS, PAGE), 1)

    def cache_scores(i):
        page = jnp.minimum(table[0, i], LIVE_PAGES - 1)
        raw = dot_t(qb[pl.ds(pl.multiple_of(i * RPS, RPS), RPS)], kbuf[page])
        sc[pl.ds(pl.multiple_of(i * RPS, RPS), RPS)] = jnp.where(lane < lens[g * SLOTS + i], raw * SCALE, -jnp.inf)

    def some_scores(n, _):
        for j in range(6):
            cache_scores(n * 6 + j)
        return 0

    lax.fori_loop(0, LIVE // 6, some_scores, 0)

    part = 96

    def soft(n, _):
        at = pl.ds(pl.multiple_of(n * part, part), part)
        a, b = sc[at], sn[at]
        top = jnp.max(jnp.maximum(a, b), axis=1, keepdims=True)
        ea, eb = jnp.exp(a - top), jnp.exp(b - top)
        inv = 1.0 / jnp.sum(ea + eb, axis=1, keepdims=True)
        pc[at] = (ea * inv).astype(BF16)
        pn[at] = (eb * inv).astype(BF16)
        return 0

    lax.fori_loop(0, live_rows // part, soft, 0)

    land_copy.wait()
    for n in range(3):
        ext[n, ROWS:ROWS + 16] = land_dst[n]
    r, c = iota((32, 256), 0), iota((32, 256), 1)
    m, s = r >> 4, r & 3
    early = s < pick(m, mv_arr)
    mv_pick = one_hot((early & (c == s * SLOTS + pick(m, mv_row))) | (~early & (c == ROWS + m * 4 + s)))
    spread = dot(mv_pick, ext[0])
    r, c = iota((32, FEAT), 0), iota((32, FEAT), 1)
    qm = jnp.where((c >> 7) == ((r >> 2) & 3), spread, 0.0).astype(BF16)
    qb[live_rows:] = qm
    r, c = iota((32, 256), 0), iota((32, 256), 1)
    m, s = r >> 4, r & 3
    arr, row = pick(m, mv_arr), pick(m, mv_row)
    u_own, u_land = c >> 5, c & 3
    ok_own = (c < ROWS) & ((c & 31) == row) & (u_own < arr) & (u_own <= s)
    ok_land = (c >= ROWS) & (c < ROWS + 8) & (((c >> 2) & 1) == m) & (u_land >= arr) & (u_land <= s)
    sm = jnp.where(ok_own | ok_land, dot_t(qm, ext[1]) * SCALE, -jnp.inf)
    mv_page = [[jnp.minimum(table[j, mv_row[m]], LIVE_PAGES - 1) for j in range(MAXP)] for m in range(2)]
    for m in range(2):
        q_one = qb[live_rows + m * RPS:live_rows + (m + 1) * RPS]
        for j in range(MAXP):
            raw = dot_t(q_one, kbuf[mv_page[m][j]])
            scm[m * RPS:(m + 1) * RPS, j * PAGE:(j + 1) * PAGE] = jnp.where(
                lane + j * PAGE < lens[g * SLOTS + mv_row[m]], raw * SCALE, -jnp.inf)
    a = scm[...]
    top = jnp.maximum(jnp.max(a, axis=1, keepdims=True), jnp.max(sm, axis=1, keepdims=True))
    ea, eb = jnp.exp(a - top), jnp.exp(sm - top)
    inv = 1.0 / (jnp.sum(ea, axis=1, keepdims=True) + jnp.sum(eb, axis=1, keepdims=True))
    scm[...] = ea * inv
    for cp in v_copies:
        cp.wait()
    om_new = dot((eb * inv).astype(BF16), ext[2])
    c, r = iota((RPS, FEAT), 1), iota((RPS, FEAT), 0)
    diag = (c >> 7) == (r >> 2)
    for m in range(2):
        acc = om_new[m * RPS:(m + 1) * RPS]
        for j in range(MAXP):
            acc = acc + dot(scm[m * RPS:(m + 1) * RPS, j * PAGE:(j + 1) * PAGE].astype(BF16), vbuf[mv_page[m][j]])
        ob[live_rows + m * RPS:live_rows + (m + 1) * RPS] = jnp.where(diag, acc, 0.0).astype(BF16)
    r, c = iota((16, 32), 0), iota((16, 32), 1)
    gather = one_hot(((c >> 4) == (r >> 2)) & ((c & 3) == (r & 3)))
    moved_src[...] = dot(gather, ob[live_rows:]).astype(BF16)
    moved_copy = pltpu.make_async_remote_copy(
        src_ref=moved_src, dst_ref=moved_dst, send_sem=moved_sem.at[0], recv_sem=moved_sem.at[1],
        device_id=x_peer, device_id_type=MESH)
    moved_copy.start()

    on[...] = dot(pn[...], ext[2, 0:ROWS])

    def some_values(n, _):
        for j in range(6):
            i = n * 6 + j
            at = pl.ds(pl.multiple_of(i * RPS, RPS), RPS)
            page = jnp.minimum(table[0, i], LIVE_PAGES - 1)
            acc = on[at] + dot(pc[at], vbuf[page])
            ob[at] = jnp.where(diag, acc, 0.0).astype(BF16)
        return 0

    lax.fori_loop(0, LIVE // 6, some_values, 0)

    r, c = iota((ROWS, 512), 0), iota((ROWS, 512), 1)
    slot, step = r & 31, r >> 5
    src, src_step, m = c >> 4, c & 3, (c >> 4) - LIVE
    stays = (src < LIVE) & (slot == src) & (slot != mv_slot[0]) & (slot != mv_slot[1])
    moves = (src >= LIVE) & (slot == pick(m, mv_slot)) & (step < pick(m, mv_arr))
    keep = one_hot((step == src_step) & (stays | moves))
    total = dot(keep, ob[...])
    moved_copy.wait()
    r, c = iota((ROWS, 16), 0), iota((ROWS, 16), 1)
    slot, step, m = r & 31, r >> 5, (c >> 2) & 1
    lands = (c < 8) & (slot == LIVE + m) & (step == (c & 3)) & (step >= pick(m, in_arr)) & (pick(m, in_slot) < LIVE)
    attn[...] = (total + dot(one_hot(lands), moved_dst[...])).astype(BF16)

    low = iota((64, HD), 1) < 64
    core0 = core == 0

    def project(k):
        for cp in w_copies(k):
            cp.wait()
        res = dot(attn[...], wbuf[k])
        mid_a, mid_b = res[0:64, HD:2 * HD], res[64:ROWS, HD:2 * HD]
        left = jnp.where(low, mid_a, pltpu.roll(mid_b, 64, 1))
        right = jnp.where(low, pltpu.roll(mid_a, 64, 1), mid_b)
        own[k, 0:ROWS] = res[:, 0:HD]
        own[k, ROWS:UNIT] = jnp.where(core0, left, right)
        core_src[k, 0:ROWS] = res[:, 2 * HD:].astype(BF16)
        core_src[k, ROWS:UNIT] = jnp.where(core0, right, left).astype(BF16)

    def core_copy(k):
        return pltpu.make_async_remote_copy(
            src_ref=core_src.at[k], dst_ref=core_dst.at[k], send_sem=core_ssem.at[k], recv_sem=core_rsem.at[k],
            device_id=sibling, device_id_type=MESH)

    def y_copy(k):
        return pltpu.make_async_remote_copy(
            src_ref=y_src.at[k], dst_ref=y_dst.at[k], send_sem=y_ssem.at[k], recv_sem=y_rsem.at[k],
            device_id=y_peer, device_id_type=MESH)

    def z_copy(k):
        return pltpu.make_async_remote_copy(
            src_ref=z_src.at[k], dst_ref=z_dst.at[k], send_sem=z_ssem.at[k], recv_sem=z_rsem.at[k],
            device_id=z_peer(Z_ORDER[k]), device_id_type=MESH)

    def away(k):
        core_copy(k).wait_recv()
        y_src[k] = (own[k] + core_dst[k].astype(F32)).astype(BF16)
        y_copy(k).start()

    for k in range(NZ):
        project(k)
        core_copy(k).start()
        if k >= 2:
            away(k - 2)
    away(NZ - 2)
    away(NZ - 1)
    for k in range(NZ):
        project(NZ + k)
        core_copy(NZ + k).start()

    def home(k):
        core_copy(NZ + k).wait_recv()
        y_copy(k).wait_recv()
        return own[NZ + k] + core_dst[NZ + k].astype(F32) + y_dst[k].astype(F32)

    for k in range(NZ - 1):
        z_src[k] = home(k).astype(BF16)
        z_copy(k).start()
    result = home(NZ - 1)
    for k in range(NZ - 1):
        z_copy(k).wait_recv()
        result = result + z_dst[k].astype(F32)

    side = result[0:ROWS]
    mid = result[ROWS:UNIT]
    first = iota((ROWS, HD), 1) < 64
    mid_left = jnp.concatenate([mid, pltpu.roll(mid, 64, 1)], 0)
    turned = pltpu.roll(side, 64, 1)
    one = jnp.where(core0, side, jnp.where(first, mid_left, turned))
    two = jnp.where(core0, mid_left, turned)
    out[:, 0:HD] = one.astype(BF16)
    out[:, HD:UNIT] = two[:, 0:64].astype(BF16)

    for k in range(2 * NZ):
        core_copy(k).wait_send()
    for k in range(NZ):
        y_copy(k).wait_send()
    for k in range(NZ - 1):
        z_copy(k).wait_send()


def per_device(kv, qkv, w, table, lens, plan):
    vmem, sems = pltpu.VMEM, pltpu.SemaphoreType.DMA
    hbm, smem = pl.BlockSpec(memory_space=pl.ANY), pl.BlockSpec(memory_space=pltpu.SMEM)
    unit = (UNIT, HD)
    res = pl.pallas_call(
        kernel,
        out_shape=jax.ShapeDtypeStruct((ROWS, UNIT), BF16),
        in_specs=[hbm, hbm, hbm, smem, smem, smem],
        out_specs=pl.BlockSpec(memory_space=pltpu.VMEM),
        scratch_shapes=[
            vmem((LIVE_PAGES, PAGE, FEAT), BF16), vmem((LIVE_PAGES, PAGE, FEAT), BF16), vmem((2 * NZ, FEAT, FEAT), BF16),
            vmem((3, 256, FEAT), BF16), vmem((3, 16, FEAT), BF16), vmem((3, 16, FEAT), BF16),
            vmem((16, FEAT), BF16), vmem((16, FEAT), BF16),
            vmem((512, FEAT), BF16), vmem((LIVE * RPS, PAGE), F32), vmem((LIVE * RPS, ROWS), F32),
            vmem((32, MAXP * PAGE), F32), vmem((32, 256), F32),
            vmem((LIVE * RPS, PAGE), BF16), vmem((LIVE * RPS, ROWS), BF16), vmem((LIVE * RPS, FEAT), F32),
            vmem((512, FEAT), BF16), vmem((ROWS, FEAT), BF16),
            vmem((2 * NZ,) + unit, F32), vmem((2 * NZ,) + unit, BF16), vmem((2 * NZ,) + unit, BF16),
            vmem((NZ,) + unit, BF16), vmem((NZ,) + unit, BF16),
            vmem((NZ - 1,) + unit, BF16), vmem((NZ - 1,) + unit, BF16),
            sems((CHUNKS,)), sems((CHUNKS,)), sems((2 * NZ, 3)), sems, sems((2,)), sems((2,)),
            sems((2 * NZ,)), sems((2 * NZ,)), sems((NZ,)), sems((NZ,)), sems((NZ - 1,)), sems((NZ - 1,)),
        ],
        compiler_params=pltpu.CompilerParams(collective_id=0, has_side_effects=True, vmem_limit_bytes=60 << 20),
    )(kv, qkv.reshape(3, ROWS, FEAT), w, table.T, lens, plan.T)
    return res.reshape(STEPS, SLOTS, UNIT)


def solution(mesh):
    return jax.shard_map(
        per_device,
        mesh=mesh,
        in_specs=(P(None, "grp", None, "head"), P(None, None, "grp", "head"), P("head", None), P("grp", None), P(), P()),
        out_specs=P(None, "grp", "head"),
        check_vma=False,
    )
```

time: 208 us -> 39.8 us (0.19)
  the two profiles are of different devices: /device:TPU:2 before, /device:TPU:1 now
where the time goes in v1:
time: 39.8 us; the launch traced here: 39.6 us
  Pallas kernels  38.2 us (96%)
  local copies, waits for them, and re-layouts  1.47 us (4%)
    pallas_call x1, Pallas kernels, per_device(): pl.pallas_call(kernel, out_shape=jax.ShapeDtypeStruct((ROWS, UNIT), BF16)...  38.2 us
    unnamed x1, local copies, waits for them, and re-layouts  1.47 us

profile of v1, /device:TPU:1, one launch (start us, length us, event | category | flops | bytes accessed | tf_op | source)
XLA Modules:
  0.0 39.6 jit_solution(5871499377514877958)
XLA Ops:
  0.0 38.2 %shard_map.64 = bf16[128,192]{1,0:T(8,128)(2,1)} custom-call(bf16[2,44,128,384]{3,2,1,0:T(8,128)(2,1)} %kv.1, bf16[3,128,384]{2,1,0:T(8,128)(2,1)} %bitcast.4, bf16[384,6144]{1,0:T(8,128)(2,1)} %w.1, s32[4,32]{1,0:T(4,128)} %bitcast.6, s32[256]{0:T(256)} %lens.1, s32[2,16]{1,0:T(2,128)} %bitcast.7), custom_call_target="tpu_custom_call" | custom-call | tf_op jit(solution)/shard_map/pallas_call | solution.py:310
  38.2 1.5 %copy.8 = bf16[4,32,192]{2,1,0:T(8,128)(2,1)} copy(bf16[4,32,192]{2,1,0:T(8,128)(2,1)} %bitcast.5) | data formatting | bytes 98304

commit v2 on v1

v2 whole, which is shorter than its diff:
```python
import jax
import jax.numpy as jnp
from jax import lax
from jax.experimental import pallas as pl
from jax.experimental.pallas import tpu as pltpu
from jax.sharding import PartitionSpec as P

MESH = pl.DeviceIdType.MESH
HD = 128
HEADS = 3
FEAT = HEADS * HD
STEPS = 4
SLOTS = 32
LIVE = 30
LIVE_PAGES = 36
PAGE = 128
MAXP = 4
ROWS = STEPS * SLOTS
RPS = 16
CHUNKS = 4
NZ = 8
UNIT = 192
F32 = jnp.float32
BF16 = jnp.bfloat16
SCALE = HD ** -0.5


def iota(shape, dim):
    return lax.broadcasted_iota(jnp.int32, shape, dim)


def one_hot(cond):
    return jnp.where(cond, 1.0, 0.0).astype(BF16)


def dot(a, b):
    return jnp.dot(a, b, preferred_element_type=F32)


def dot_t(a, b):
    return lax.dot_general(a, b, (((1,), (1,)), ((), ())), preferred_element_type=F32)


def kernel(kv, qkv, w, table_in, lens_in, plan_in, out,
           table, lens, plan, kbuf, vbuf, wbuf, ext, land_src, land_dst, moved_src, moved_dst,
           qb, sc, sn, scm, pc, pn, on, ob, attn, attn_c,
           own, y_src, y_dst, z_src, z_dst, own_c, yc_src, yc_dst, zc_src, zc_dst,
           i_sem, k_sem, v_sem, w_sem, q_sem, land_sem, moved_sem, core_sem, core_c_sem,
           wp_ssem, wp_rsem, y_ssem, y_rsem, z_ssem, z_rsem, yc_sem, zc_ssem, zc_rsem):
    g = lax.axis_index("grp")
    h = lax.axis_index("head")
    yh, z, core = h // 16, lax.rem(h // 2, NZ), lax.rem(h, 2)
    sibling = (g, h + 1 - 2 * core)
    y_peer = (g, lax.rem(h + 16, 32))
    pair = lax.rem(g + 4, 8)
    x_peer = (pair, h)

    def z_device(t):
        return (g, yh * 16 + t * 2 + core)

    def z_at(k):
        return z if k == NZ - 1 else k + jnp.where(z > k, 0, 1)

    q_copy = pltpu.make_async_copy(qkv, ext.at[:, pl.ds(0, ROWS)], q_sem)
    q_copy.start()
    i_copies = [pltpu.make_async_copy(src, dst, i_sem.at[n])
                for n, (src, dst) in enumerate(((table_in, table), (lens_in, lens), (plan_in, plan)))]
    for cp in i_copies:
        cp.start()
    per = LIVE_PAGES // CHUNKS

    def page_copies(which, buf, sem):
        return [pltpu.make_async_copy(kv.at[which, pl.ds(n * per, per)], buf.at[pl.ds(n * per, per)], sem.at[n])
                for n in range(CHUNKS)]

    k_copies = page_copies(0, kbuf, k_sem)
    v_copies = page_copies(1, vbuf, v_sem)
    for cp in k_copies + v_copies:
        cp.start()

    barrier = pltpu.get_barrier_semaphore()
    peers = [sibling, y_peer] + [z_device(z_at(k)) for k in range(NZ - 1)] + [x_peer]
    for peer in peers:
        pl.semaphore_signal(barrier, inc=1, device_id=peer, device_id_type=MESH)

    def w_columns(k, c):
        b = (1 - yh) if k < NZ else yh
        return w.at[:, pl.ds(pl.multiple_of((b * NZ + z_at(k % NZ)) * FEAT + c * HD, HD), 2 * HD)]

    def w_copy(k):
        return pltpu.make_async_copy(w_columns(k, core), wbuf.at[k, pl.ds(0, FEAT)], w_sem.at[k])

    def w_push(k):
        return pltpu.make_async_remote_copy(
            src_ref=w_columns(k, 1 - core), dst_ref=wbuf.at[k, pl.ds(FEAT, FEAT)], send_sem=wp_ssem.at[k], recv_sem=wp_rsem.at[k],
            device_id=sibling, device_id_type=MESH)

    q_copy.wait()
    r, c = iota((16, ROWS), 0), iota((16, ROWS), 1)
    land_pick = one_hot((r < 8) & (c == (r & 3) * SLOTS + LIVE + (r >> 2)))
    for n in range(3):
        land_src[n] = dot(land_pick, ext[n, 0:ROWS]).astype(BF16)
        ext[n, ROWS + 16:256] = jnp.zeros((112, FEAT), BF16)

    for cp in i_copies:
        cp.wait()
    mv_slot = [plan[0, g * 2 + m] for m in range(2)]
    mv_arr = [plan[1, g * 2 + m] for m in range(2)]
    in_slot = [plan[0, pair * 2 + m] for m in range(2)]
    in_arr = [plan[1, pair * 2 + m] for m in range(2)]
    mv_row = [jnp.minimum(s, LIVE - 1) for s in mv_slot]

    def pick(m, values):
        return jnp.where(m == 0, values[0], values[1])

    live_rows = LIVE * RPS
    r, c = iota((live_rows, ROWS), 0), iota((live_rows, ROWS), 1)
    q_pick = one_hot(c == (r & 3) * SLOTS + (r >> 4))
    spread = dot(q_pick, ext[0, 0:ROWS])
    r, c = iota((live_rows, FEAT), 0), iota((live_rows, FEAT), 1)
    qb[0:live_rows] = jnp.where((c >> 7) == ((r >> 2) & 3), spread, 0.0).astype(BF16)

    r, c = iota((live_rows, ROWS), 0), iota((live_rows, ROWS), 1)
    raw = dot_t(qb[0:live_rows], ext[1, 0:ROWS])
    sn[...] = jnp.where(((c & 31) == (r >> 4)) & ((c >> 5) <= (r & 3)), raw * SCALE, -jnp.inf)

    pl.semaphore_wait(barrier, len(peers))
    land_copy = pltpu.make_async_remote_copy(
        src_ref=land_src, dst_ref=land_dst, send_sem=land_sem.at[0], recv_sem=land_sem.at[1],
        device_id=x_peer, device_id_type=MESH)
    land_copy.start()
    for k in range(2 * NZ):
        w_push(k).start()

    for cp in k_copies:
        cp.wait()
    for k in range(2 * NZ):
        w_copy(k).start()
    lane = iota((RPS, PAGE), 1)

    def cache_scores(i):
        page = jnp.minimum(table[0, i], LIVE_PAGES - 1)
        raw = dot_t(qb[pl.ds(pl.multiple_of(i * RPS, RPS), RPS)], kbuf[page])
        sc[pl.ds(pl.multiple_of(i * RPS, RPS), RPS)] = jnp.where(lane < lens[g * SLOTS + i], raw * SCALE, -jnp.inf)

    def some_scores(n, _):
        for j in range(6):
            cache_scores(n * 6 + j)
        return 0

    lax.fori_loop(0, LIVE // 6, some_scores, 0)

    part = 96

    def soft(n, _):
        at = pl.ds(pl.multiple_of(n * part, part), part)
        a, b = sc[at], sn[at]
        top = jnp.max(jnp.maximum(a, b), axis=1, keepdims=True)
        ea, eb = jnp.exp(a - top), jnp.exp(b - top)
        inv = 1.0 / jnp.sum(ea + eb, axis=1, keepdims=True)
        pc[at] = (ea * inv).astype(BF16)
        pn[at] = (eb * inv).astype(BF16)
        return 0

    lax.fori_loop(0, live_rows // part, soft, 0)

    for cp in v_copies:
        cp.wait()
    c, r = iota((RPS, FEAT), 1), iota((RPS, FEAT), 0)
    diag = (c >> 7) == (r >> 2)
    on[...] = dot(pn[...], ext[2, 0:ROWS])

    def some_values(n, _):
        for j in range(6):
            i = n * 6 + j
            at = pl.ds(pl.multiple_of(i * RPS, RPS), RPS)
            page = jnp.minimum(table[0, i], LIVE_PAGES - 1)
            acc = on[at] + dot(pc[at], vbuf[page])
            ob[at] = jnp.where(diag, acc, 0.0).astype(BF16)
        return 0

    lax.fori_loop(0, LIVE // 6, some_values, 0)

    r, c = iota((ROWS, live_rows), 0), iota((ROWS, live_rows), 1)
    slot = r & 31
    keep = ((r >> 5) == (c & 3)) & (slot == (c >> 4)) & (slot != mv_slot[0]) & (slot != mv_slot[1])
    attn[:, 0:FEAT] = dot(one_hot(keep), ob[0:live_rows]).astype(BF16)
    attn_copy = pltpu.make_async_remote_copy(
        src_ref=attn.at[:, pl.ds(0, FEAT)], dst_ref=attn.at[:, pl.ds(FEAT, FEAT)], send_sem=core_sem.at[0], recv_sem=core_sem.at[1],
        device_id=sibling, device_id_type=MESH)
    attn_copy.start()

    land_copy.wait_recv()
    for n in range(3):
        ext[n, ROWS:ROWS + 16] = land_dst[n]
    r, c = iota((32, 256), 0), iota((32, 256), 1)
    m, s = r >> 4, r & 3
    early = s < pick(m, mv_arr)
    mv_pick = one_hot((early & (c == s * SLOTS + pick(m, mv_row))) | (~early & (c == ROWS + m * 4 + s)))
    spread = dot(mv_pick, ext[0])
    r, c = iota((32, FEAT), 0), iota((32, FEAT), 1)
    qm = jnp.where((c >> 7) == ((r >> 2) & 3), spread, 0.0).astype(BF16)
    qb[live_rows:] = qm
    r, c = iota((32, 256), 0), iota((32, 256), 1)
    m, s = r >> 4, r & 3
    arr, row = pick(m, mv_arr), pick(m, mv_row)
    u_own, u_land = c >> 5, c & 3
    ok_own = (c < ROWS) & ((c & 31) == row) & (u_own < arr) & (u_own <= s)
    ok_land = (c >= ROWS) & (c < ROWS + 8) & (((c >> 2) & 1) == m) & (u_land >= arr) & (u_land <= s)
    sm = jnp.where(ok_own | ok_land, dot_t(qm, ext[1]) * SCALE, -jnp.inf)
    mv_page = [[jnp.minimum(table[j, mv_row[m]], LIVE_PAGES - 1) for j in range(MAXP)] for m in range(2)]
    for m in range(2):
        q_one = qb[live_rows + m * RPS:live_rows + (m + 1) * RPS]
        for j in range(MAXP):
            raw = dot_t(q_one, kbuf[mv_page[m][j]])
            scm[m * RPS:(m + 1) * RPS, j * PAGE:(j + 1) * PAGE] = jnp.where(
                lane + j * PAGE < lens[g * SLOTS + mv_row[m]], raw * SCALE, -jnp.inf)
    a = scm[...]
    top = jnp.maximum(jnp.max(a, axis=1, keepdims=True), jnp.max(sm, axis=1, keepdims=True))
    ea, eb = jnp.exp(a - top), jnp.exp(sm - top)
    inv = 1.0 / (jnp.sum(ea, axis=1, keepdims=True) + jnp.sum(eb, axis=1, keepdims=True))
    scm[...] = ea * inv
    om_new = dot((eb * inv).astype(BF16), ext[2])
    for m in range(2):
        acc = om_new[m * RPS:(m + 1) * RPS]
        for j in range(MAXP):
            acc = acc + dot(scm[m * RPS:(m + 1) * RPS, j * PAGE:(j + 1) * PAGE].astype(BF16), vbuf[mv_page[m][j]])
        ob[live_rows + m * RPS:live_rows + (m + 1) * RPS] = jnp.where(diag, acc, 0.0).astype(BF16)
    r, c = iota((16, 32), 0), iota((16, 32), 1)
    gather = one_hot(((c >> 4) == (r >> 2)) & ((c & 3) == (r & 3)))
    moved = dot(gather, ob[live_rows:])
    moved_src[...] = moved.astype(BF16)
    moved_copy = pltpu.make_async_remote_copy(
        src_ref=moved_src, dst_ref=moved_dst, send_sem=moved_sem.at[0], recv_sem=moved_sem.at[1],
        device_id=x_peer, device_id_type=MESH)
    moved_copy.start()

    low = iota((64, HD), 1) < 64
    core0 = core == 0

    def project(k):
        w_copy(k).wait()
        w_push(k).wait_recv()
        res = dot(attn[...], wbuf[k])
        one, two = res[:, 0:HD], res[:, HD:2 * HD]
        left = jnp.where(low, two[0:64], pltpu.roll(two[64:ROWS], 64, 1))
        right = jnp.where(low, pltpu.roll(one[0:64], 64, 1), one[64:ROWS])
        return jnp.where(core0, one, two), jnp.where(core0, left, right)

    def y_copy(k):
        return pltpu.make_async_remote_copy(
            src_ref=y_src.at[k], dst_ref=y_dst.at[k], send_sem=y_ssem.at[k], recv_sem=y_rsem.at[k],
            device_id=y_peer, device_id_type=MESH)

    def z_copy(k, slot):
        return pltpu.make_async_remote_copy(
            src_ref=z_src.at[k], dst_ref=z_dst.at[slot], send_sem=z_ssem.at[k], recv_sem=z_rsem.at[slot],
            device_id=z_device(z_at(k)), device_id_type=MESH)

    def slot_at(k):
        return z - jnp.where(z > k, 1, 0)

    def send_home(k):
        y_copy(k).wait_recv()
        z_src[k] = (own[k] + y_dst[k].astype(F32)).astype(BF16)
        z_copy(k, slot_at(k)).start()

    attn_copy.wait_recv()
    for k in range(NZ):
        side, mid = project(k)
        y_src[k, 0:ROWS] = side.astype(BF16)
        y_src[k, ROWS:UNIT] = mid.astype(BF16)
        y_copy(k).start()
    for k in range(NZ):
        own[k, 0:ROWS], own[k, ROWS:UNIT] = project(NZ + k)

    moved_copy.wait_recv()
    r = iota((16, FEAT), 0)
    m, s = (r >> 2) & 1, r & 3
    leaves = (r < 8) & (s < pick(m, mv_arr))
    lands = (r < 8) & (s >= pick(m, in_arr)) & (pick(m, in_slot) < LIVE)
    attn_c[:, 0:FEAT] = jnp.where(leaves, moved, jnp.where(lands, moved_dst[...].astype(F32), 0.0)).astype(BF16)
    attn_c_copy = pltpu.make_async_remote_copy(
        src_ref=attn_c.at[:, pl.ds(0, FEAT)], dst_ref=attn_c.at[:, pl.ds(FEAT, FEAT)],
        send_sem=core_c_sem.at[0], recv_sem=core_c_sem.at[1], device_id=sibling, device_id_type=MESH)
    attn_c_copy.start()
    yc_copy = pltpu.make_async_remote_copy(
        src_ref=yc_src, dst_ref=yc_dst, send_sem=yc_sem.at[0], recv_sem=yc_sem.at[1], device_id=y_peer, device_id_type=MESH)

    def zc_copy(k, slot):
        return pltpu.make_async_remote_copy(
            src_ref=zc_src.at[k], dst_ref=zc_dst.at[slot], send_sem=zc_ssem.at[k], recv_sem=zc_rsem.at[slot],
            device_id=z_device(z_at(k)), device_id_type=MESH)

    def project_c(k):
        res = dot(attn_c[...], wbuf[k])
        one, two = res[0:8, 0:HD], res[0:8, HD:2 * HD]
        return jnp.concatenate([jnp.where(core0, one, two), jnp.where(core0, two, one)], 0)

    for k in range(2):
        send_home(k)
    attn_c_copy.wait_recv()
    for k in range(NZ):
        yc_src[k] = project_c(k).astype(BF16)
    yc_copy.start()
    for k in range(2, 4):
        send_home(k)
    for k in range(NZ):
        own_c[k] = project_c(NZ + k)
    for k in range(4, 6):
        send_home(k)
    yc_copy.wait_recv()
    own_c[...] = own_c[...] + yc_dst[...].astype(F32)
    for k in range(NZ - 1):
        zc_src[k] = own_c[k].astype(BF16)
    for k in range(NZ - 1):
        zc_copy(k, slot_at(k)).start()
    send_home(6)
    y_copy(NZ - 1).wait_recv()
    total = own[NZ - 1] + y_dst[NZ - 1].astype(F32)
    total_c = own_c[NZ - 1]
    for k in range(NZ - 1):
        z_copy(0, k).wait_recv()
        total = total + z_dst[k].astype(F32)
    for k in range(NZ - 1):
        zc_copy(0, k).wait_recv()
        total_c = total_c + zc_dst[k].astype(F32)

    def columns(side, middle, first):
        turned = pltpu.roll(side, 64, 1)
        return jnp.where(core0, side, jnp.where(first, middle, turned)), jnp.where(core0, middle, turned)

    mid = total[ROWS:UNIT]
    one, two = columns(total[0:ROWS], jnp.concatenate([mid, pltpu.roll(mid, 64, 1)], 0), iota((ROWS, HD), 1) < 64)
    mid = total_c[8:16]
    one_c, two_c = columns(total_c[0:8], jnp.where(core0, mid, pltpu.roll(mid, 64, 1)), iota((8, HD), 1) < 64)
    rest = jnp.zeros((8, HD), F32)
    r, c = iota((ROWS, 16), 0), iota((ROWS, 16), 1)
    slot, step, m = r & 31, r >> 5, (c >> 2) & 1
    lands = (slot == LIVE + m) & (step >= pick(m, in_arr)) & (pick(m, in_slot) < LIVE)
    leaves = (slot == pick(m, mv_slot)) & (step < pick(m, mv_arr))
    place = one_hot((c < 8) & (step == (c & 3)) & (lands | leaves))
    one = one + dot(place, jnp.concatenate([one_c, rest], 0).astype(BF16))
    two = two + dot(place, jnp.concatenate([two_c, rest], 0).astype(BF16))
    out[:, 0:HD] = one.astype(BF16)
    out[:, HD:UNIT] = two[:, 0:64].astype(BF16)

    for cp in (land_copy, attn_copy, moved_copy, attn_c_copy, yc_copy):
        cp.wait_send()
    for k in range(2 * NZ):
        w_push(k).wait_send()
    for k in range(NZ):
        y_copy(k).wait_send()
    for k in range(NZ - 1):
        z_copy(k, 0).wait_send()
        zc_copy(k, 0).wait_send()


def per_device(kv, qkv, w, table, lens, plan):
    vmem, sems = pltpu.VMEM, pltpu.SemaphoreType.DMA
    hbm = pl.BlockSpec(memory_space=pltpu.HBM)
    unit = (UNIT, HD)
    res = pl.pallas_call(
        kernel,
        out_shape=jax.ShapeDtypeStruct((ROWS, UNIT), BF16),
        in_specs=[hbm] * 6,
        out_specs=pl.BlockSpec(memory_space=pltpu.VMEM),
        scratch_shapes=[
            pltpu.SMEM((MAXP, SLOTS), jnp.int32), pltpu.SMEM(lens.shape, jnp.int32), pltpu.SMEM(plan.shape[::-1], jnp.int32),
            vmem((LIVE_PAGES, PAGE, FEAT), BF16), vmem((LIVE_PAGES, PAGE, FEAT), BF16), vmem((2 * NZ, 2 * FEAT, 2 * HD), BF16),
            vmem((3, 256, FEAT), BF16), vmem((3, 16, FEAT), BF16), vmem((3, 16, FEAT), BF16),
            vmem((16, FEAT), BF16), vmem((16, FEAT), BF16),
            vmem((512, FEAT), BF16), vmem((LIVE * RPS, PAGE), F32), vmem((LIVE * RPS, ROWS), F32), vmem((32, MAXP * PAGE), F32),
            vmem((LIVE * RPS, PAGE), BF16), vmem((LIVE * RPS, ROWS), BF16), vmem((LIVE * RPS, FEAT), F32),
            vmem((512, FEAT), BF16), vmem((ROWS, 2 * FEAT), BF16), vmem((16, 2 * FEAT), BF16),
            vmem((NZ,) + unit, F32), vmem((NZ,) + unit, BF16), vmem((NZ,) + unit, BF16),
            vmem((NZ - 1,) + unit, BF16), vmem((NZ - 1,) + unit, BF16),
            vmem((NZ, 16, HD), F32), vmem((NZ, 16, HD), BF16), vmem((NZ, 16, HD), BF16),
            vmem((NZ - 1, 16, HD), BF16), vmem((NZ - 1, 16, HD), BF16),
            sems((3,)), sems((CHUNKS,)), sems((CHUNKS,)), sems((2 * NZ,)), sems, sems((2,)), sems((2,)), sems((2,)), sems((2,)),
            sems((2 * NZ,)), sems((2 * NZ,)), sems((NZ,)), sems((NZ,)), sems((NZ - 1,)), sems((NZ - 1,)),
            sems((2,)), sems((NZ - 1,)), sems((NZ - 1,)),
        ],
        compiler_params=pltpu.CompilerParams(collective_id=0, has_side_effects=True, vmem_limit_bytes=60 << 20),
    )(kv, qkv.reshape(3, ROWS, FEAT), w, table.T, lens, plan.T)
    return res.reshape(STEPS, SLOTS, UNIT)


def solution(mesh):
    return jax.shard_map(
        per_device,
        mesh=mesh,
        in_specs=(P(None, "grp", None, "head"), P(None, None, "grp", "head"), P("head", None), P("grp", None), P(), P()),
        out_specs=P(None, "grp", "head"),
        check_vma=False,
    )
```

time: 39.8 us -> 35.5 us (0.89)
  the two profiles are of different devices: /device:TPU:1 before, /device:TPU:2 now
where the time goes in v2:
time: 35.5 us; the launch traced here: 35.2 us
  Pallas kernels  33.7 us (95%)
  local copies, waits for them, and re-layouts  1.47 us (4%)
    pallas_call x1, Pallas kernels, per_device(): pl.pallas_call(kernel, out_shape=jax.ShapeDtypeStruct((ROWS, UNIT), BF16)...  33.7 us
    unnamed x1, local copies, waits for them, and re-layouts  1.47 us

profile of v2, /device:TPU:2, one launch (start us, length us, event | category | flops | bytes accessed | tf_op | source)
XLA Modules:
  0.0 35.2 jit_solution(10035843656240439170)
XLA Ops:
  0.0 33.7 %shard_map.64 = bf16[128,192]{1,0:T(8,128)(2,1)} custom-call(bf16[2,44,128,384]{3,2,1,0:T(8,128)(2,1)} %kv.1, bf16[3,128,384]{2,1,0:T(8,128)(2,1)} %bitcast.4, bf16[384,6144]{1,0:T(8,128)(2,1)} %w.1, s32[4,32]{1,0:T(4,128)} %bitcast.6, s32[256]{0:T(256)} %lens_in.1, s32[2,16]{1,0:T(2,128)} %bitcast.7), custom_call_target="tpu_custom_call" | custom-call | tf_op jit(solution)/shard_map/pallas_call | solution.py:363
  33.7 1.5 %copy.8 = bf16[4,32,192]{2,1,0:T(8,128)(2,1)} copy(bf16[4,32,192]{2,1,0:T(8,128)(2,1)} %bitcast.5) | data formatting | bytes 98304

commit v3 on v2

--- a/solution.py
+++ b/solution.py
@@ -19,6 +19,10 @@
 RPS = 16
 CHUNKS = 4
 NZ = 8
+Y_FIRST = 5
+FIRST_Z = (0, 1)
+Z_ORDER = [[t for t in FIRST_Z if t != n] + sorted((t for t in range(NZ) if t != n and t not in FIRST_Z),
+                                                   key=lambda t: -min((t - n) % NZ, (n - t) % NZ)) for n in range(NZ)]
 UNIT = 192
 F32 = jnp.float32
 BF16 = jnp.bfloat16
@@ -44,9 +48,9 @@
 def kernel(kv, qkv, w, table_in, lens_in, plan_in, out,
            table, lens, plan, kbuf, vbuf, wbuf, ext, land_src, land_dst, moved_src, moved_dst,
            qb, sc, sn, scm, pc, pn, on, ob, attn, attn_c,
-           own, y_src, y_dst, z_src, z_dst, own_c, yc_src, yc_dst, zc_src, zc_dst,
-           i_sem, k_sem, v_sem, w_sem, q_sem, land_sem, moved_sem, core_sem, core_c_sem,
-           wp_ssem, wp_rsem, y_ssem, y_rsem, z_ssem, z_rsem, yc_sem, zc_ssem, zc_rsem):
+           own, y_src, y_dst, z_src, z_dst, yc_src, yc_dst, zc_src, zc_dst,
+           i_sem, k_sem, v_sem, w_sem, q_sem, land_sem, moved_ssem, moved_rsem, core_sem,
+           wp_ssem, wp_rsem, y_ssem, y_rsem, z_ssem, z_rsem, yc_ssem, yc_rsem, zc_ssem, zc_rsem, above_sem):
     g = lax.axis_index("grp")
     h = lax.axis_index("head")
     yh, z, core = h // 16, lax.rem(h // 2, NZ), lax.rem(h, 2)
@@ -59,7 +63,12 @@
         return (g, yh * 16 + t * 2 + core)
 
     def z_at(k):
-        return z if k == NZ - 1 else k + jnp.where(z > k, 0, 1)
+        if k == NZ - 1:
+            return z
+        t = Z_ORDER[0][k]
+        for n in range(1, NZ):
+            t = jnp.where(z == n, Z_ORDER[n][k], t)
+        return t
 
     q_copy = pltpu.make_async_copy(qkv, ext.at[:, pl.ds(0, ROWS)], q_sem)
     q_copy.start()
@@ -79,9 +88,20 @@
         cp.start()
 
     barrier = pltpu.get_barrier_semaphore()
-    peers = [sibling, y_peer] + [z_device(z_at(k)) for k in range(NZ - 1)] + [x_peer]
-    for peer in peers:
+    x_sibling = (pair, h + 1 - 2 * core)
+    near = (sibling, y_peer, x_peer, x_sibling)
+    for peer in near:
         pl.semaphore_signal(barrier, inc=1, device_id=peer, device_id_type=MESH)
+
+    def greet_above(t, _):
+        pl.semaphore_signal(barrier, inc=1, device_id=z_device(t), device_id_type=MESH)
+        return 0
+
+    def answer_below(t, _):
+        pl.semaphore_signal(above_sem, inc=1, device_id=z_device(t), device_id_type=MESH)
+        return 0
+
+    lax.fori_loop(z + 1, NZ, greet_above, 0)
 
     def w_columns(k, c):
         b = (1 - yh) if k < NZ else yh
@@ -120,17 +140,18 @@
     r, c = iota((live_rows, FEAT), 0), iota((live_rows, FEAT), 1)
     qb[0:live_rows] = jnp.where((c >> 7) == ((r >> 2) & 3), spread, 0.0).astype(BF16)
 
-    r, c = iota((live_rows, ROWS), 0), iota((live_rows, ROWS), 1)
-    raw = dot_t(qb[0:live_rows], ext[1, 0:ROWS])
-    sn[...] = jnp.where(((c & 31) == (r >> 4)) & ((c >> 5) <= (r & 3)), raw * SCALE, -jnp.inf)
-
-    pl.semaphore_wait(barrier, len(peers))
+    pl.semaphore_wait(barrier, len(near) + z)
     land_copy = pltpu.make_async_remote_copy(
         src_ref=land_src, dst_ref=land_dst, send_sem=land_sem.at[0], recv_sem=land_sem.at[1],
         device_id=x_peer, device_id_type=MESH)
     land_copy.start()
     for k in range(2 * NZ):
         w_push(k).start()
+    lax.fori_loop(0, z, answer_below, 0)
+
+    r, c = iota((live_rows, ROWS), 0), iota((live_rows, ROWS), 1)
+    raw = dot_t(qb[0:live_rows], ext[1, 0:ROWS])
+    sn[...] = jnp.where(((c & 31) == (r >> 4)) & ((c >> 5) <= (r & 3)), raw * SCALE, -jnp.inf)
 
     for cp in k_copies:
         cp.wait()
@@ -140,17 +161,13 @@
 
     def cache_scores(i):
         page = jnp.minimum(table[0, i], LIVE_PAGES - 1)
-        raw = dot_t(qb[pl.ds(pl.multiple_of(i * RPS, RPS), RPS)], kbuf[page])
-        sc[pl.ds(pl.multiple_of(i * RPS, RPS), RPS)] = jnp.where(lane < lens[g * SLOTS + i], raw * SCALE, -jnp.inf)
-
-    def some_scores(n, _):
-        for j in range(6):
-            cache_scores(n * 6 + j)
-        return 0
-
-    lax.fori_loop(0, LIVE // 6, some_scores, 0)
-
-    part = 96
+        raw = dot_t(qb[i * RPS:(i + 1) * RPS], kbuf[page])
+        sc[i * RPS:(i + 1) * RPS] = jnp.where(lane < lens[g * SLOTS + i], raw * SCALE, -jnp.inf)
+
+    for i in range(LIVE):
+        cache_scores(i)
+
+    part = 240
 
     def soft(n, _):
         at = pl.ds(pl.multiple_of(n * part, part), part)
@@ -170,16 +187,11 @@
     diag = (c >> 7) == (r >> 2)
     on[...] = dot(pn[...], ext[2, 0:ROWS])
 
-    def some_values(n, _):
-        for j in range(6):
-            i = n * 6 + j
-            at = pl.ds(pl.multiple_of(i * RPS, RPS), RPS)
-            page = jnp.minimum(table[0, i], LIVE_PAGES - 1)
-            acc = on[at] + dot(pc[at], vbuf[page])
-            ob[at] = jnp.where(diag, acc, 0.0).astype(BF16)
-        return 0
-
-    lax.fori_loop(0, LIVE // 6, some_values, 0)
+    for i in range(LIVE):
+        at = pl.ds(i * RPS, RPS)
+        page = jnp.minimum(table[0, i], LIVE_PAGES - 1)
+        acc = on[at] + dot(pc[at], vbuf[page])
+        ob[at] = jnp.where(diag, acc, 0.0).astype(BF16)
 
     r, c = iota((ROWS, live_rows), 0), iota((ROWS, live_rows), 1)
     slot = r & 31
@@ -230,10 +242,11 @@
     gather = one_hot(((c >> 4) == (r >> 2)) & ((c & 3) == (r & 3)))
     moved = dot(gather, ob[live_rows:])
     moved_src[...] = moved.astype(BF16)
-    moved_copy = pltpu.make_async_remote_copy(
-        src_ref=moved_src, dst_ref=moved_dst, send_sem=moved_sem.at[0], recv_sem=moved_sem.at[1],
-        device_id=x_peer, device_id_type=MESH)
-    moved_copy.start()
+    moved_copies = [pltpu.make_async_remote_copy(
+        src_ref=moved_src, dst_ref=moved_dst.at[n], send_sem=moved_ssem.at[n], recv_sem=moved_rsem.at[n],
+        device_id=peer, device_id_type=MESH) for n, peer in enumerate((x_peer, x_sibling, sibling))]
+    for cp in moved_copies:
+        cp.start()
 
     low = iota((64, HD), 1) < 64
     core0 = core == 0
@@ -258,7 +271,7 @@
             device_id=z_device(z_at(k)), device_id_type=MESH)
 
     def slot_at(k):
-        return z - jnp.where(z > k, 1, 0)
+        return z - jnp.where(z > z_at(k), 1, 0)
 
     def send_home(k):
         y_copy(k).wait_recv()
@@ -270,22 +283,25 @@
         side, mid = project(k)
         y_src[k, 0:ROWS] = side.astype(BF16)
         y_src[k, ROWS:UNIT] = mid.astype(BF16)
-        y_copy(k).start()
+        if k < Y_FIRST:
+            y_copy(k).start()
     for k in range(NZ):
         own[k, 0:ROWS], own[k, ROWS:UNIT] = project(NZ + k)
 
-    moved_copy.wait_recv()
+    for cp in moved_copies:
+        cp.wait_recv()
     r = iota((16, FEAT), 0)
     m, s = (r >> 2) & 1, r & 3
     leaves = (r < 8) & (s < pick(m, mv_arr))
     lands = (r < 8) & (s >= pick(m, in_arr)) & (pick(m, in_slot) < LIVE)
-    attn_c[:, 0:FEAT] = jnp.where(leaves, moved, jnp.where(lands, moved_dst[...].astype(F32), 0.0)).astype(BF16)
-    attn_c_copy = pltpu.make_async_remote_copy(
-        src_ref=attn_c.at[:, pl.ds(0, FEAT)], dst_ref=attn_c.at[:, pl.ds(FEAT, FEAT)],
-        send_sem=core_c_sem.at[0], recv_sem=core_c_sem.at[1], device_id=sibling, device_id_type=MESH)
-    attn_c_copy.start()
-    yc_copy = pltpu.make_async_remote_copy(
-        src_ref=yc_src, dst_ref=yc_dst, send_sem=yc_sem.at[0], recv_sem=yc_sem.at[1], device_id=y_peer, device_id_type=MESH)
+    for n, mine in enumerate((moved, moved_dst[2].astype(F32))):
+        attn_c[:, n * FEAT:(n + 1) * FEAT] = jnp.where(
+            leaves, mine, jnp.where(lands, moved_dst[n].astype(F32), 0.0)).astype(BF16)
+
+    def yc_copy(k, slot):
+        return pltpu.make_async_remote_copy(
+            src_ref=yc_src.at[k], dst_ref=yc_dst.at[slot], send_sem=yc_ssem.at[k], recv_sem=yc_rsem.at[slot],
+            device_id=(g, (1 - yh) * 16 + z_at(k) * 2 + core), device_id_type=MESH)
 
     def zc_copy(k, slot):
         return pltpu.make_async_remote_copy(
@@ -297,34 +313,35 @@
         one, two = res[0:8, 0:HD], res[0:8, HD:2 * HD]
         return jnp.concatenate([jnp.where(core0, one, two), jnp.where(core0, two, one)], 0)
 
-    for k in range(2):
-        send_home(k)
-    attn_c_copy.wait_recv()
+    @pl.when(z < NZ - 1)
+    def _():
+        pl.semaphore_wait(above_sem, NZ - 1 - z)
+
+    send_home(0)
     for k in range(NZ):
         yc_src[k] = project_c(k).astype(BF16)
-    yc_copy.start()
-    for k in range(2, 4):
-        send_home(k)
-    for k in range(NZ):
-        own_c[k] = project_c(NZ + k)
-    for k in range(4, 6):
-        send_home(k)
-    yc_copy.wait_recv()
-    own_c[...] = own_c[...] + yc_dst[...].astype(F32)
+    for k in range(NZ):
+        yc_copy(k, z).start()
+    for k in range(Y_FIRST, NZ):
+        y_copy(k).start()
     for k in range(NZ - 1):
-        zc_src[k] = own_c[k].astype(BF16)
+        zc_src[k] = project_c(NZ + k).astype(BF16)
     for k in range(NZ - 1):
         zc_copy(k, slot_at(k)).start()
-    send_home(6)
+    total_c = project_c(2 * NZ - 1)
+    for k in range(1, NZ - 1):
+        send_home(k)
     y_copy(NZ - 1).wait_recv()
     total = own[NZ - 1] + y_dst[NZ - 1].astype(F32)
-    total_c = own_c[NZ - 1]
     for k in range(NZ - 1):
         z_copy(0, k).wait_recv()
         total = total + z_dst[k].astype(F32)
     for k in range(NZ - 1):
         zc_copy(0, k).wait_recv()
         total_c = total_c + zc_dst[k].astype(F32)
+    for k in range(NZ):
+        yc_copy(0, k).wait_recv()
+        total_c = total_c + yc_dst[k].astype(F32)
 
     def columns(side, middle, first):
         turned = pltpu.roll(side, 64, 1)
@@ -345,12 +362,13 @@
     out[:, 0:HD] = one.astype(BF16)
     out[:, HD:UNIT] = two[:, 0:64].astype(BF16)
 
-    for cp in (land_copy, attn_copy, moved_copy, attn_c_copy, yc_copy):
+    for cp in [land_copy, attn_copy] + moved_copies:
         cp.wait_send()
     for k in range(2 * NZ):
         w_push(k).wait_send()
     for k in range(NZ):
         y_copy(k).wait_send()
+        yc_copy(k, 0).wait_send()
     for k in range(NZ - 1):
         z_copy(k, 0).wait_send()
         zc_copy(k, 0).wait_send()
@@ -369,17 +387,17 @@
             pltpu.SMEM((MAXP, SLOTS), jnp.int32), pltpu.SMEM(lens.shape, jnp.int32), pltpu.SMEM(plan.shape[::-1], jnp.int32),
             vmem((LIVE_PAGES, PAGE, FEAT), BF16), vmem((LIVE_PAGES, PAGE, FEAT), BF16), vmem((2 * NZ, 2 * FEAT, 2 * HD), BF16),
             vmem((3, 256, FEAT), BF16), vmem((3, 16, FEAT), BF16), vmem((3, 16, FEAT), BF16),
-            vmem((16, FEAT), BF16), vmem((16, FEAT), BF16),
+            vmem((16, FEAT), BF16), vmem((3, 16, FEAT), BF16),
             vmem((512, FEAT), BF16), vmem((LIVE * RPS, PAGE), F32), vmem((LIVE * RPS, ROWS), F32), vmem((32, MAXP * PAGE), F32),
             vmem((LIVE * RPS, PAGE), BF16), vmem((LIVE * RPS, ROWS), BF16), vmem((LIVE * RPS, FEAT), F32),
             vmem((512, FEAT), BF16), vmem((ROWS, 2 * FEAT), BF16), vmem((16, 2 * FEAT), BF16),
             vmem((NZ,) + unit, F32), vmem((NZ,) + unit, BF16), vmem((NZ,) + unit, BF16),
             vmem((NZ - 1,) + unit, BF16), vmem((NZ - 1,) + unit, BF16),
-            vmem((NZ, 16, HD), F32), vmem((NZ, 16, HD), BF16), vmem((NZ, 16, HD), BF16),
+            vmem((NZ, 16, HD), BF16), vmem((NZ, 16, HD), BF16),
             vmem((NZ - 1, 16, HD), BF16), vmem((NZ - 1, 16, HD), BF16),
-            sems((3,)), sems((CHUNKS,)), sems((CHUNKS,)), sems((2 * NZ,)), sems, sems((2,)), sems((2,)), sems((2,)), sems((2,)),
+            sems((3,)), sems((CHUNKS,)), sems((CHUNKS,)), sems((2 * NZ,)), sems, sems((2,)), sems((3,)), sems((3,)), sems((2,)),
             sems((2 * NZ,)), sems((2 * NZ,)), sems((NZ,)), sems((NZ,)), sems((NZ - 1,)), sems((NZ - 1,)),
-            sems((2,)), sems((NZ - 1,)), sems((NZ - 1,)),
+            sems((NZ,)), sems((NZ,)), sems((NZ - 1,)), sems((NZ - 1,)), pltpu.SemaphoreType.REGULAR,
         ],
         compiler_params=pltpu.CompilerParams(collective_id=0, has_side_effects=True, vmem_limit_bytes=60 << 20),
     )(kv, qkv.reshape(3, ROWS, FEAT), w, table.T, lens, plan.T)

time: 35.5 us -> 33.2 us (0.935)
  Pallas kernels: 33.7 us -> 31.6 us
    pallas_call x1, Pallas kernels: 33.7 us -> 31.6 us  [per_device(): pl.pallas_call(kernel, out_shape=jax.ShapeDtypeStruct((ROWS, UNIT), BF16)...]
where the time goes in v3:
time: 33.2 us; the launch traced here: 33.1 us
  Pallas kernels  31.6 us (95%)
  local copies, waits for them, and re-layouts  1.47 us (4%)
    pallas_call x1, Pallas kernels, per_device(): pl.pallas_call(kernel, out_shape=jax.ShapeDtypeStruct((ROWS, UNIT), BF16)...  31.6 us
    unnamed x1, local copies, waits for them, and re-layouts  1.47 us

profile of v3, /device:TPU:2, one launch (start us, length us, event | category | flops | bytes accessed | tf_op | source)
XLA Modules:
  0.0 33.1 jit_solution(18419570907639592893)
XLA Ops:
  0.0 31.6 %shard_map.64 = bf16[128,192]{1,0:T(8,128)(2,1)} custom-call(bf16[2,44,128,384]{3,2,1,0:T(8,128)(2,1)} %kv.1, bf16[3,128,384]{2,1,0:T(8,128)(2,1)} %bitcast.4, bf16[384,6144]{1,0:T(8,128)(2,1)} %w.1, s32[4,32]{1,0:T(4,128)} %bitcast.6, s32[256]{0:T(256)} %lens_in.1, s32[2,16]{1,0:T(2,128)} %bitcast.7), custom_call_target="tpu_custom_call" | custom-call | tf_op jit(solution)/shard_map/pallas_call | solution.py:381
  31.6 1.5 %copy.8 = bf16[4,32,192]{2,1,0:T(8,128)(2,1)} copy(bf16[4,32,192]{2,1,0:T(8,128)(2,1)} %bitcast.5) | data formatting | bytes 98304

commit v4 on v3

--- a/solution.py
+++ b/solution.py
@@ -17,9 +17,8 @@
 MAXP = 4
 ROWS = STEPS * SLOTS
 RPS = 16
-CHUNKS = 4
+CHUNKS = 1
 NZ = 8
-Y_FIRST = 5
 FIRST_Z = (0, 1)
 Z_ORDER = [[t for t in FIRST_Z if t != n] + sorted((t for t in range(NZ) if t != n and t not in FIRST_Z),
                                                    key=lambda t: -min((t - n) % NZ, (n - t) % NZ)) for n in range(NZ)]
@@ -283,8 +282,7 @@
         side, mid = project(k)
         y_src[k, 0:ROWS] = side.astype(BF16)
         y_src[k, ROWS:UNIT] = mid.astype(BF16)
-        if k < Y_FIRST:
-            y_copy(k).start()
+        y_copy(k).start()
     for k in range(NZ):
         own[k, 0:ROWS], own[k, ROWS:UNIT] = project(NZ + k)
 
@@ -322,8 +320,6 @@
         yc_src[k] = project_c(k).astype(BF16)
     for k in range(NZ):
         yc_copy(k, z).start()
-    for k in range(Y_FIRST, NZ):
-        y_copy(k).start()
     for k in range(NZ - 1):
         zc_src[k] = project_c(NZ + k).astype(BF16)
     for k in range(NZ - 1):

time: 33.2 us -> 32.5 us (0.979); the launches traced: 33.1 us -> 32 us
  Pallas kernels: 31.6 us -> 30.5 us
    pallas_call x1, Pallas kernels: 31.6 us -> 30.5 us  [per_device(): pl.pallas_call(kernel, out_shape=jax.ShapeDtypeStruct((ROWS, UNIT), BF16)...]
where the time goes in v4:
time: 32.5 us; the launch traced here: 32 us
  Pallas kernels  30.5 us (94%)
  local copies, waits for them, and re-layouts  1.47 us (5%)
    pallas_call x1, Pallas kernels, per_device(): pl.pallas_call(kernel, out_shape=jax.ShapeDtypeStruct((ROWS, UNIT), BF16)...  30.5 us
    unnamed x1, local copies, waits for them, and re-layouts  1.47 us

profile of v4, /device:TPU:2, one launch (start us, length us, event | category | flops | bytes accessed | tf_op | source)
XLA Modules:
  0.0 32.0 jit_solution(3590931456771648561)
XLA Ops:
  0.0 30.5 %shard_map.64 = bf16[128,192]{1,0:T(8,128)(2,1)} custom-call(bf16[2,44,128,384]{3,2,1,0:T(8,128)(2,1)} %kv.1, bf16[3,128,384]{2,1,0:T(8,128)(2,1)} %bitcast.4, bf16[384,6144]{1,0:T(8,128)(2,1)} %w.1, s32[4,32]{1,0:T(4,128)} %bitcast.6, s32[256]{0:T(256)} %lens_in.1, s32[2,16]{1,0:T(2,128)} %bitcast.7), custom_call_target="tpu_custom_call" | custom-call | tf_op jit(solution)/shard_map/pallas_call | solution.py:377
  30.5 1.5 %copy.8 = bf16[4,32,192]{2,1,0:T(8,128)(2,1)} copy(bf16[4,32,192]{2,1,0:T(8,128)(2,1)} %bitcast.5) | data formatting | bytes 98304

commit v5 on v4

--- a/solution.py
+++ b/solution.py
@@ -327,11 +327,6 @@
     total_c = project_c(2 * NZ - 1)
     for k in range(1, NZ - 1):
         send_home(k)
-    y_copy(NZ - 1).wait_recv()
-    total = own[NZ - 1] + y_dst[NZ - 1].astype(F32)
-    for k in range(NZ - 1):
-        z_copy(0, k).wait_recv()
-        total = total + z_dst[k].astype(F32)
     for k in range(NZ - 1):
         zc_copy(0, k).wait_recv()
         total_c = total_c + zc_dst[k].astype(F32)
@@ -343,8 +338,6 @@
         turned = pltpu.roll(side, 64, 1)
         return jnp.where(core0, side, jnp.where(first, middle, turned)), jnp.where(core0, middle, turned)
 
-    mid = total[ROWS:UNIT]
-    one, two = columns(total[0:ROWS], jnp.concatenate([mid, pltpu.roll(mid, 64, 1)], 0), iota((ROWS, HD), 1) < 64)
     mid = total_c[8:16]
     one_c, two_c = columns(total_c[0:8], jnp.where(core0, mid, pltpu.roll(mid, 64, 1)), iota((8, HD), 1) < 64)
     rest = jnp.zeros((8, HD), F32)
@@ -353,8 +346,16 @@
     lands = (slot == LIVE + m) & (step >= pick(m, in_arr)) & (pick(m, in_slot) < LIVE)
     leaves = (slot == pick(m, mv_slot)) & (step < pick(m, mv_arr))
     place = one_hot((c < 8) & (step == (c & 3)) & (lands | leaves))
-    one = one + dot(place, jnp.concatenate([one_c, rest], 0).astype(BF16))
-    two = two + dot(place, jnp.concatenate([two_c, rest], 0).astype(BF16))
+    add_one = dot(place, jnp.concatenate([one_c, rest], 0).astype(BF16))
+    add_two = dot(place, jnp.concatenate([two_c, rest], 0).astype(BF16))
+    y_copy(NZ - 1).wait_recv()
+    total = own[NZ - 1] + y_dst[NZ - 1].astype(F32)
+    for k in range(NZ - 1):
+        z_copy(0, k).wait_recv()
+        total = total + z_dst[k].astype(F32)
+    mid = total[ROWS:UNIT]
+    one, two = columns(total[0:ROWS], jnp.concatenate([mid, pltpu.roll(mid, 64, 1)], 0), iota((ROWS, HD), 1) < 64)
+    one, two = one + add_one, two + add_two
     out[:, 0:HD] = one.astype(BF16)
     out[:, HD:UNIT] = two[:, 0:64].astype(BF16)
 

time: 32.5 us -> 32.5 us (level)
  no operation moved by 1% of the time
where the time goes in v5:
time: 32.5 us; the launch traced here: 32.1 us
  Pallas kernels  30.7 us (94%)
  local copies, waits for them, and re-layouts  1.47 us (5%)
    pallas_call x1, Pallas kernels, per_device(): pl.pallas_call(kernel, out_shape=jax.ShapeDtypeStruct((ROWS, UNIT), BF16)...  30.7 us
    unnamed x1, local copies, waits for them, and re-layouts  1.47 us

profile of v5, /device:TPU:2, one launch (start us, length us, event | category | flops | bytes accessed | tf_op | source)
XLA Modules:
  0.0 32.1 jit_solution(8454181671510102380)
XLA Ops:
  0.0 30.7 %shard_map.64 = bf16[128,192]{1,0:T(8,128)(2,1)} custom-call(bf16[2,44,128,384]{3,2,1,0:T(8,128)(2,1)} %kv.1, bf16[3,128,384]{2,1,0:T(8,128)(2,1)} %bitcast.4, bf16[384,6144]{1,0:T(8,128)(2,1)} %w.1, s32[4,32]{1,0:T(4,128)} %bitcast.6, s32[256]{0:T(256)} %lens_in.1, s32[2,16]{1,0:T(2,128)} %bitcast.7), custom_call_target="tpu_custom_call" | custom-call | tf_op jit(solution)/shard_map/pallas_call | solution.py:378
  30.7 1.5 %copy.8 = bf16[4,32,192]{2,1,0:T(8,128)(2,1)} copy(bf16[4,32,192]{2,1,0:T(8,128)(2,1)} %bitcast.5) | data formatting | bytes 98304
